TPU v7x, 512 devices: a whole 4x8x8 slice. The times are simulated.
512 devices in a mesh: row: 4 (over x), col: 16 (over y, core), layer: 8 (over z).
Axes of the slice: x: 4, y: 8, z: 8, core: 2. Of those that a mesh axis runs over, the one named last changes fastest.
Arguments:
- iterate_rows: bfloat16 [8, 8192, 8192], P('layer', 'col', 'row'), may hold values from -0.078125 to 0.078125
- square_slab: bfloat16 [8, 8192, 2048], P('layer', 'col', 'row'), may hold values from -1 to 1
- row_pattern: int32 [8, 16, 16], P('layer', 'col'), may hold values from 0 to 1, as said below
- slab_pattern: int32 [8, 16, 4], P('layer', 'col', 'row'), may hold values 0 or 1
- fill_counts: int32 [8, 16], P('layer', 'col'), may hold values from 256 to 512
- iterate_slab: float32 [8192, 2048], P(('col', 'layer'), 'row'), may hold values from -2.5 to 2.5
Outputs:
- updated: float32 [8192, 2048], P(('col', 'layer'), 'row')
Inputs may be any that keep to these rules, and one draw needn't show every extreme that they name: `row_pattern`: each aligned run of 4 tiles along the last dimension holds 0 to 2 occupied tiles; for every layer and tile row one run holds exactly 2.
All inputs are finite; a program needn't handle non-finite values. No bound on the sum of `slab_pattern` on one device may be relied on, other than what follows from the above.
Results may differ from a plain program's by a relative error of at most 0.0003.
Values may be sent and summed in bfloat16 or wider, within the bound.
A program may use at most 64 MiB of HBM per device.

v0:
```python
import jax
import jax.numpy as jnp
from jax import lax
from jax.sharding import PartitionSpec as P


def body(iterate_rows, square_slab, row_pattern, slab_pattern, fill_counts, iterate_slab):
    width = square_slab.shape[2]
    per_device = square_slab.shape[1] // width
    per_block = iterate_rows.shape[2] // width
    row_count = lax.axis_size("row")
    all_tiles = per_block * row_count
    tile_weights = row_pattern[0, 0].astype(jnp.bfloat16)
    row_tiles = lax.all_gather(iterate_rows, "row", axis=2, tiled=True)[0].reshape(
        width, all_tiles, width
    )
    offsets = jnp.arange(width, dtype=jnp.int32)
    live = (offsets[None, :] < fill_counts[0][:, None]) & (slab_pattern[0, :, 0][:, None] > 0)
    masked = square_slab[0].reshape(per_device, width, width) * live[:, :, None].astype(
        jnp.bfloat16
    )
    right = lax.all_gather(masked, "col", axis=0, tiled=True) * tile_weights[:, None, None]
    partial_sum = jnp.einsum("itk,tkj->ij", row_tiles, right, preferred_element_type=jnp.float32)
    product = lax.psum_scatter(partial_sum, "layer", scatter_dimension=0, tiled=True)
    return 1.5 * iterate_slab - 0.5 * product


def solution(mesh):
    return jax.shard_map(
        body,
        mesh=mesh,
        in_specs=(
            P("layer", "col", "row"),
            P("layer", "col", "row"),
            P("layer", "col", None),
            P("layer", "col", "row"),
            P("layer", "col"),
            P(("col", "layer"), "row"),
        ),
        out_specs=P(("col", "layer"), "row"),
        check_vma=False,
    )
```

profile of v0, /device:TPU:1, one launch (start us, length us, event | category | flops | bytes accessed | tf_op | source)
XLA Modules:
  0.0 221.3 jit_solution(11259334123964255787)
XLA Ops:
  6.5 0.0 all-gather.5.cloned.1.call-start
  6.5 3.9 %copy.20 = bf16[1,512,2048]{1,2,0:T(8,128)(2,1)} copy(bf16[1,512,2048]{2,1,0:T(8,128)(2,1)} %param.6) | data formatting | bytes 4194304 | tf_op args[0]
  10.5 0.0 all-gather.5.cloned.1.call-update
  10.5 0.0 all-gather.3.cloned.1.call-start
  11.8 2.0 broadcast_multiply_fusion
  13.8 0.0 all-gather.3.cloned.1.call-update
  13.8 0.0 reduce-scatter.4.cloned.1.call-start
  13.9 0.7 convert_bitcast_fusion
  14.5 90.0 %all-gather.5.cloned.1.call-done = bf16[1,512,8192]{1,2,0:T(8,128)(2,1)} async-done(((bf16[1,512,2048]{1,2,0:T(8,128)(2,1)}), bf16[1,512,8192]{1,2,0:T(8,128)(2,1)}) %all-gather.5.cloned.1.call-update) | async-done | bytes 8388624 | tf_op jit(solution)/shard_map/all_gather | solution.py:14
  104.6 61.8 %all-gather.3.cloned.1.call-done = bf16[16,512,512]{2,1,0:T(8,128)(2,1)} async-done(((bf16[1,512,512]{2,1,0:T(8,128)(2,1)}), bf16[16,512,512]{2,1,0:T(8,128)(2,1)}) %all-gather.3.cloned.1.call-update) | async-done | bytes 8388624 | tf_op jit(solution)/shard_map/all_gather | solution.py:22
  166.4 0.0 copy-start
  166.4 9.5 %fusion.3 = f32[512,512]{0,1:T(8,128)S(1)} fusion(bf16[512,16,512]{0,2,1:T(8,128)(2,1)} %bitcast.12, bf16[16,512,512]{2,1,0:T(8,128)(2,1)} %all-gather.3.cloned.1.call-done, bf16[16]{0:T(256)(128)(2,1)S(1)} %convert_bitcast_fusion), kind=kOutput, calls=%fused_computation.3 | convolution fusion | flops 4299161600 | bytes 17825824 | tf_op jit(solution)/shard_map/itk,tkj->ij/dot_general | solution.py:23
  175.9 1.3 copy.26
  177.2 0.0 reduce-scatter.4.cloned.1.call-update
  177.3 35.9 %reduce-scatter.4.cloned.1.call-done = f32[64,512]{1,0:T(8,128)} async-done(((f32[512,512]{1,0:T(8,128)}), f32[64,512]{1,0:T(8,128)}) %reduce-scatter.4.cloned.1.call-update) | async-done | bytes 131088 | tf_op jit(solution)/shard_map/reduce_scatter | solution.py:24
  213.2 0.0 copy-done
  213.2 1.6 multiply_subtract_fusion
  (1 shorter events, 0.0 us)
Async XLA Ops:
  6.5 98.0 %all-gather.5.cloned.1.call-start = ((), (), s32[]{:S(2)}) async-start(), calls=%async_computation.2 | async-start | bytes 10485760 | tf_op jit(solution)/shard_map/all_gather | solution.py:14
  10.5 155.9 %all-gather.3.cloned.1.call-start = ((), (), s32[]{:S(2)}) async-start(), calls=%async_computation.1 | async-start | bytes 8912896 | tf_op jit(solution)/shard_map/all_gather | solution.py:22
  13.8 199.3 %reduce-scatter.4.cloned.1.call-start = ((), (), s32[]{:S(2)}) async-start(), calls=%async_computation.3 | async-start | bytes 1179648 | tf_op jit(solution)/shard_map/reduce_scatter | solution.py:24
  166.4 46.8 %copy-start = (f32[64,512]{1,0:T(8,128)S(1)}, f32[64,512]{1,0:T(8,128)}, u32[]{:S(2)}) copy-start(f32[64,512]{1,0:T(8,128)} %param.11) | copy-start | bytes 393220
Sparse Core Ops, SparseCore 0:
  10.6 93.9 all-gather.4
  106.7 59.6 all-gather.2
  177.4 35.7 reduce-scatter.3
where the time goes:
time: 226 us; the launch traced here: 221 us
  waiting for transfers between devices  188 us (83%)
  between operations  14.4 us (6%)
  matrix products  9.55 us (4%)
  local copies, waits for them, and re-layouts  5.22 us (2%)
  other arithmetic  4.22 us (2%)
    all_gather x1, waiting for transfers between devices, body(): lax.all_gather(iterate_rows, 'row', axis=2, tiled=True)[0]  90 us
    all_gather x1, waiting for transfers between devices, body(): lax.all_gather(masked, 'col', axis=0, tiled=True)  61.8 us
    reduce_scatter x1, waiting for transfers between devices, body(): lax.psum_scatter(partial_sum, 'layer', scatter_dimension=0, tiled=True)  35.9 us
    dot_general x1, matrix products, body(): jnp.einsum('itk,tkj->ij', row_tiles, right, preferred_element_type=jnp.fl...  9.55 us
    unnamed x4, local copies, waits for them, and re-layouts  5.22 us
  transfers between devices with their start and end apart: 3, of which 3 were waited for; matrix products, arithmetic and copies ran while one was open for 1% of the time, Pallas kernels for 0%

commit v1 on v0

v1 whole, which is shorter than its diff:
```python
import functools

import jax
import jax.numpy as jnp
from jax import lax
from jax.experimental import pallas as pl
from jax.experimental.pallas import tpu as pltpu
from jax.sharding import PartitionSpec as P

MESH = pl.DeviceIdType.MESH
TILE = 512
RUNS = 4
PER_RUN = 4
SLOTS = 2
TILES = 16
CHIPS = 8
LAYERS = 8
CHUNKS = 4
LANES = TILE // CHUNKS
SUBS = 2
DEPTH = TILE // SUBS
STAGES = 4
OWNED = TILE // LAYERS
STAGE_ROWS = TILE // STAGES
OFFSETS = (4, 3, 5, 2, 6, 1, 7, 0)
HOPS = {("R", 0): 4, ("R", 1): 3, ("L", 0): 3, ("L", 1): 4}

SLOT_US = 1.4
LATENCY_US = 2.0
STAGE_US = 8.0


def ring_order(direction):
    streams = [(q, s) for q in range(CHUNKS) for s in range(SUBS)]
    done = {u: 0 for u in streams}
    ready = {u: 0 for u in streams}
    order, slot = [], 0
    while any(done[u] < HOPS[direction, u[1]] for u in streams):
        left = [u for u in streams if done[u] < HOPS[direction, u[1]]]
        active = [u for u in left if ready[u] <= slot]
        if active:
            u = active[0]
            done[u] += 1
            ready[u] = slot + 3
            order.append((slot, u[0], u[1], done[u]))
        slot += 1
    return order


def build_events():
    events = []
    arrival = {}
    last = [0.0] * CHUNKS
    for direction in ("R", "L"):
        for slot, q, s, hop in ring_order(direction):
            start = slot * SLOT_US
            events.append((start - SLOT_US, 1, ("send", direction, q, s, hop)))
            arrival[direction, q, s, hop] = start + SLOT_US + LATENCY_US
    for (direction, q, s, hop), when in arrival.items():
        last[q] = max(last[q], when)
        if hop == HOPS[direction, s]:
            events.append((when, 0, ("land", direction, q, s, hop)))
    for q in range(CHUNKS):
        events.append((q * 8 * SLOT_US - SLOT_US, 2, ("share", q)))
    for h in range(STAGES):
        events.append(((h - 1.5) * STAGE_US, 3, ("left", h)))
    for q in range(CHUNKS):
        for h in range(STAGES):
            when = max(last[q] + 1.0, (h + 1) * STAGE_US + LATENCY_US)
            events.append((when, 4, ("block", q, h)))
    order = sorted(events, key=lambda e: (max(e[0], 0.0), e[1], e[0]))
    return [e[2] for e in order]


def kernel(
    rows_hbm, slab_hbm, pattern_hbm, kept_hbm, fill_hbm, out_ref,
    rows, slab, pattern, kept, fill, left, right0, right1, right2, right3, partial, landed,
    in_sem, scalar_sem, left_send, left_recv, ring_send, ring_recv, pair_send, pair_recv, sum_send, sum_recv,
):
    right = (right0, right1, right2, right3)
    r, c, l = (lax.axis_index(name) for name in ("row", "col", "layer"))
    core = lax.rem(c, 2)
    sibling = (r, c + 1 - 2 * core, l)
    ring = {"R": (r, lax.rem(c + 2, TILES), l), "L": (r, lax.rem(c + TILES - 2, TILES), l)}
    row_mates = [(lax.rem(r + o, RUNS), c, l) for o in range(1, RUNS)]
    layer_mates = [(r, c, lax.rem(l + o, LAYERS)) for o in OFFSETS[:-1]]

    slab_copy = pltpu.make_async_copy(slab_hbm.at[0], slab, in_sem.at[PER_RUN])
    scalar_copies = [
        pltpu.make_async_copy(pattern_hbm, pattern, scalar_sem.at[0]),
        pltpu.make_async_copy(kept_hbm, kept, scalar_sem.at[1]),
        pltpu.make_async_copy(fill_hbm, fill, scalar_sem.at[2]),
    ]
    tile_copies = [
        pltpu.make_async_copy(rows_hbm.at[0, :, pl.ds(t * TILE, TILE)], rows.at[t], in_sem.at[t])
        for t in range(PER_RUN)
    ]
    for copy in scalar_copies + [slab_copy] + tile_copies:
        copy.start()

    barrier = pltpu.get_barrier_semaphore()
    mates = layer_mates + row_mates + [ring["R"], ring["L"], sibling]
    for mate in mates:
        pl.semaphore_signal(barrier, inc=1, device_id=mate, device_id_type=MESH)

    for copy in scalar_copies:
        copy.wait()
    picks = []
    for g in range(RUNS):
        bits = [pattern[0, 0, g * PER_RUN + t] > 0 for t in range(PER_RUN)]
        first = jnp.where(bits[0], 0, jnp.where(bits[1], 1, jnp.where(bits[2], 2, 3)))
        final = jnp.where(bits[3], 3, jnp.where(bits[2], 2, jnp.where(bits[1], 1, 0)))
        picks.append((g * PER_RUN + first, g * PER_RUN + final))
    own = [pattern[0, 0, r * PER_RUN + t] for t in range(PER_RUN)]
    count = own[0] + own[1] + own[2] + own[3]
    own_first = jnp.where(own[0] > 0, 0, jnp.where(own[1] > 0, 1, jnp.where(own[2] > 0, 2, 3)))
    own_final = jnp.where(own[3] > 0, 3, jnp.where(own[2] > 0, 2, jnp.where(own[1] > 0, 1, 0)))

    slab_copy.wait()
    limit = jnp.where(kept[0, 0, 0] > 0, fill[0, 0], 0)
    live = lax.broadcasted_iota(jnp.int32, (TILE, LANES), 0) < limit
    for q in range(CHUNKS):
        piece = slab[:, q * LANES:(q + 1) * LANES].astype(jnp.float32)
        right[q][c] = jnp.where(live, piece, 0.0).astype(jnp.bfloat16)

    for copy in tile_copies:
        copy.wait()
    for slot, (tile, least) in enumerate(((own_first, 1), (own_final, 2))):
        weight = jnp.full((OWNED, TILE), jnp.where(count >= least, 1.0, 0.0), jnp.float32).astype(jnp.bfloat16)
        for p, o in enumerate(OFFSETS):
            first_row = pl.multiple_of(lax.rem(l + o, LAYERS) * OWNED, OWNED)
            piece = rows[tile, pl.ds(first_row, OWNED), :]
            left[p // 2, r, slot, (p % 2) * OWNED:(p % 2 + 1) * OWNED, :] = piece * weight

    pl.semaphore_wait(barrier, len(mates))

    pieces = [(d, q, s, h) for d in ("R", "L") for q in range(CHUNKS) for s in range(SUBS) for h in range(1, HOPS[d, s] + 1)]
    number = {piece: i for i, piece in enumerate(pieces)}

    def tile_of(direction, hops):
        return lax.rem(c + (TILES - 2 * hops if direction == "R" else 2 * hops), TILES)

    def hop_copy(direction, q, s, hop):
        view = right[q].at[tile_of(direction, hop - 1), pl.ds(s * DEPTH, DEPTH)]
        return pltpu.make_async_remote_copy(
            src_ref=view, dst_ref=view, send_sem=ring_send.at[0 if direction == "R" else 1],
            recv_sem=ring_recv.at[number[direction, q, s, hop]], device_id=ring[direction], device_id_type=MESH)

    def take(direction, q, s, hop):
        view = right[q].at[tile_of(direction, hop), pl.ds(s * DEPTH, DEPTH)]
        pltpu.make_async_copy(view, view, ring_recv.at[number[direction, q, s, hop]]).wait()
        pltpu.make_async_remote_copy(
            src_ref=view, dst_ref=view, send_sem=pair_send.at[q], recv_sem=pair_recv.at[q],
            device_id=sibling, device_id_type=MESH).start()

    have_left, have_right = set(), set()
    for step in build_events():
        if step[0] == "send":
            _, direction, q, s, hop = step
            if hop > 1:
                take(direction, q, s, hop - 1)
            hop_copy(direction, q, s, hop).start()
        elif step[0] == "land":
            take(*step[1:])
        elif step[0] == "share":
            view = right[step[1]].at[c]
            pltpu.make_async_remote_copy(
                src_ref=view, dst_ref=view, send_sem=pair_send.at[step[1]], recv_sem=pair_recv.at[step[1]],
                device_id=sibling, device_id_type=MESH).start()
        elif step[0] == "left":
            view = left.at[step[1], r]
            for mate in row_mates:
                pltpu.make_async_remote_copy(
                    src_ref=view, dst_ref=view, send_sem=left_send.at[step[1]], recv_sem=left_recv.at[step[1]],
                    device_id=mate, device_id_type=MESH).start()
        else:
            _, q, h = step
            if q not in have_right:
                have_right.add(q)
                view = right[q].at[pl.ds(0, TILES // 2)]
                pltpu.make_async_copy(view, view, pair_recv.at[q]).wait()
            if h not in have_left:
                have_left.add(h)
                view = left.at[h, pl.ds(0, RUNS - 1)]
                pltpu.make_async_copy(view, view, left_recv.at[h]).wait()
            total = None
            for g in range(RUNS):
                for slot in range(SLOTS):
                    term = jnp.dot(left[h, g, slot], right[q][picks[g][slot]], preferred_element_type=jnp.float32)
                    total = term if total is None else total + term
            partial[q, h] = total
            for p in (2 * h, 2 * h + 1):
                if OFFSETS[p] != 0:
                    pltpu.make_async_remote_copy(
                        src_ref=partial.at[q, h, pl.ds((p % 2) * OWNED, OWNED)], dst_ref=landed.at[q, p],
                        send_sem=sum_send.at[q], recv_sem=sum_recv.at[q],
                        device_id=layer_mates[p], device_id_type=MESH).start()

    def drain(view, sem):
        pltpu.make_async_copy(view, view, sem).wait()

    for i in range(2):
        drain(right[0].at[pl.ds(0, TILES - 2)], ring_send.at[i])
    for h in range(STAGES):
        drain(left.at[h, pl.ds(0, RUNS - 1)], left_send.at[h])
    for q in range(CHUNKS):
        drain(right[q].at[pl.ds(0, TILES // 2)], pair_send.at[q])
    for q in range(CHUNKS):
        drain(landed.at[q], sum_recv.at[q])
        total = partial[q, STAGES - 1, OWNED:, :]
        for p in range(LAYERS - 1):
            total = total + landed[q, p]
        out_ref[:, q * LANES:(q + 1) * LANES] = total
    for q in range(CHUNKS):
        drain(landed.at[q], sum_send.at[q])


def body(iterate_rows, square_slab, row_pattern, slab_pattern, fill_counts, iterate_slab):
    anywhere = pl.BlockSpec(memory_space=pl.ANY)
    dma = pltpu.SemaphoreType.DMA
    product = pl.pallas_call(
        kernel,
        out_shape=jax.ShapeDtypeStruct((OWNED, TILE), jnp.float32),
        in_specs=[anywhere] * 5,
        out_specs=pl.BlockSpec(memory_space=pltpu.VMEM),
        scratch_shapes=[
            pltpu.VMEM((PER_RUN, TILE, TILE), jnp.bfloat16),
            pltpu.VMEM((TILE, TILE), jnp.bfloat16),
            pltpu.SMEM((1, 1, TILES), jnp.int32),
            pltpu.SMEM((1, 1, 1), jnp.int32),
            pltpu.SMEM((1, 1), jnp.int32),
            pltpu.VMEM((STAGES, RUNS, SLOTS, STAGE_ROWS, TILE), jnp.bfloat16),
        ] + [pltpu.VMEM((TILES, TILE, LANES), jnp.bfloat16)] * CHUNKS + [
            pltpu.VMEM((CHUNKS, STAGES, STAGE_ROWS, LANES), jnp.float32),
            pltpu.VMEM((CHUNKS, LAYERS - 1, OWNED, LANES), jnp.float32),
            dma((PER_RUN + 1,)), dma((3,)),
            dma((STAGES,)), dma((STAGES,)),
            dma((2,)), dma((CHUNKS * SUBS * (CHIPS - 1),)),
            dma((CHUNKS,)), dma((CHUNKS,)),
            dma((CHUNKS,)), dma((CHUNKS,)),
        ],
        compiler_params=pltpu.CompilerParams(
            collective_id=0, has_side_effects=True, vmem_limit_bytes=40 << 20),
        name="sparse_product",
    )(iterate_rows, square_slab, row_pattern, slab_pattern, fill_counts)
    return 1.5 * iterate_slab - 0.5 * product


def solution(mesh):
    return jax.shard_map(
        body,
        mesh=mesh,
        in_specs=(
            P("layer", "col", "row"),
            P("layer", "col", "row"),
            P("layer", "col", None),
            P("layer", "col", "row"),
            P("layer", "col"),
            P(("col", "layer"), "row"),
        ),
        out_specs=P(("col", "layer"), "row"),
        check_vma=False,
    )
```

time: 226 us -> 87.8 us (0.39); the launches traced: 221 us -> 86.8 us
  waiting for transfers between devices: 188 us -> 0 us
  Pallas kernels: 0 us -> 81.5 us
  between operations: 14.4 us -> 1.32 us
  matrix products: 9.55 us -> 0 us
  other arithmetic: 4.22 us -> 0.68 us
    all_gather x2 -> x0, waiting for transfers between devices: 152 us -> none  [the longest x1 90 us: body(): lax.all_gather(iterate_rows, 'row', axis=2, tiled=True)[0]]
    pallas_call x0 -> x1, Pallas kernels: none -> 81.5 us  [body(): pl.pallas_call(kernel, out_shape=jax.ShapeDtypeStruct((OWNED, TILE), jnp....]
    reduce_scatter x1 -> x0, waiting for transfers between devices: 35.9 us -> none  [body(): lax.psum_scatter(partial_sum, 'layer', scatter_dimension=0, tiled=True)]
    dot_general x1 -> x0, matrix products: 9.55 us -> none  [body(): jnp.einsum('itk,tkj->ij', row_tiles, right, preferred_element_type=jnp.fl...]
    unnamed x4 -> x8, local copies, waits for them, and re-layouts: 5.22 us -> 3.28 us
  transfers between devices with their start and end apart: 3 -> 0, of which waited for: 3 -> 0; matrix products, arithmetic and copies ran while one was open for 1% -> 0% of each run, Pallas kernels for 0% -> 0%
where the time goes in v1:
time: 87.8 us; the launch traced here: 86.8 us
  Pallas kernels  81.5 us (93%)
  local copies, waits for them, and re-layouts  3.28 us (4%)
  between operations  1.32 us (2%)
    pallas_call x1, Pallas kernels, body(): pl.pallas_call(kernel, out_shape=jax.ShapeDtypeStruct((OWNED, TILE), jnp....  81.5 us
    unnamed x8, local copies, waits for them, and re-layouts  3.28 us

profile of v1, /device:TPU:1, one launch (start us, length us, event | category | flops | bytes accessed | tf_op | source)
XLA Modules:
  0.0 86.8 jit_solution(5772859128839810295)
XLA Ops:
  1.3 0.0 copy-start
  1.3 1.6 %copy-done = bf16[1,512,2048]{2,1,0:T(8,128)(2,1)S(1)} copy-done((bf16[1,512,2048]{2,1,0:T(8,128)(2,1)S(1)}, bf16[1,512,2048]{2,1,0:T(8,128)(2,1)}, u32[]{:S(2)}) %copy-start) | copy-done | bytes 2097176
  2.9 0.0 copy-start.1
  2.9 1.0 %copy-done.1 = bf16[1,512,512]{2,1,0:T(8,128)(2,1)S(1)} copy-done((bf16[1,512,512]{2,1,0:T(8,128)(2,1)S(1)}, bf16[1,512,512]{2,1,0:T(8,128)(2,1)}, u32[]{:S(2)}) %copy-start.1) | copy-done | bytes 524312
  3.9 0.0 copy-start.2
  3.9 0.7 copy-done.2
  4.6 0.0 copy-start.3
  4.6 81.5 %sparse_product.1 = f32[64,512]{1,0:T(8,128)S(1)} custom-call(bf16[1,512,2048]{2,1,0:T(8,128)(2,1)S(1)} %copy-done, bf16[1,512,512]{2,1,0:T(8,128)(2,1)S(1)} %copy-done.1, s32[1,1,16]{2,1,0:T(1,128)S(1)} %copy-done.2, s32[1,1,1]{2,1,0:T(1,128)S(6)} %copy.7.kept_hbm, s32[1,1]{1,0:T(1,128)S(6)} %copy.8.fill_hbm), custom_call_target="tpu_custom_call" | custom-call | tf_op jit(solution)/shard_map/sparse_product/pallas_call | solution.py:221
  86.1 0.0 copy-done.3
  86.2 0.7 multiply_subtract_fusion
Async XLA Ops:
  1.3 1.6 %copy-start = (bf16[1,512,2048]{2,1,0:T(8,128)(2,1)S(1)}, bf16[1,512,2048]{2,1,0:T(8,128)(2,1)}, u32[]{:S(2)}) copy-start(bf16[1,512,2048]{2,1,0:T(8,128)(2,1)} %rows_hbm.1) | copy-start | bytes 6291460
  2.9 1.0 %copy-start.1 = (bf16[1,512,512]{2,1,0:T(8,128)(2,1)S(1)}, bf16[1,512,512]{2,1,0:T(8,128)(2,1)}, u32[]{:S(2)}) copy-start(bf16[1,512,512]{2,1,0:T(8,128)(2,1)} %slab_hbm.1) | copy-start | bytes 1572868
  3.9 0.7 copy-start.2
  4.6 81.6 %copy-start.3 = (f32[64,512]{1,0:T(8,128)S(1)}, f32[64,512]{1,0:T(8,128)}, u32[]{:S(2)}) copy-start(f32[64,512]{1,0:T(8,128)} %param.11) | copy-start | bytes 393220

commit v2 on v0

v2 whole, which is shorter than its diff:
```python
import functools

import jax
import jax.numpy as jnp
from jax import lax
from jax.experimental import pallas as pl
from jax.experimental.pallas import tpu as pltpu
from jax.sharding import PartitionSpec as P

MESH = pl.DeviceIdType.MESH
TILE = 512
RUNS = 4
PER_RUN = 4
SLOTS = 2
TILES = 16
CHIPS = 8
LAYERS = 8
LANES = 128
PARTS = (128, 128, 64, 64, 64, 64)
STARTS = tuple(sum(PARTS[:p]) for p in range(len(PARTS)))
DEPTH = TILE // 2
PIECES = tuple((p, s) for p, width in enumerate(PARTS) for s in range(width // 64))
STAGES = 4
OWNED = TILE // LAYERS
STAGE_ROWS = TILE // STAGES
OFFSETS = (4, 3, 5, 2, 6, 1, 7, 0)
HOPS = {
    "R": {u: 4 - i % 2 for i, u in enumerate(PIECES)},
    "L": {u: 3 + i % 2 for i, u in enumerate(PIECES)},
}

SLOT = 1.4
LATENCY = 2.7
DEADLINES = (21, 23, 25, 33, 35, 38)
SEND_LEFT = (0.0, 0.0, 8.3, 13.8)
PASS_LEFT = (8.2, 13.7, 22.0, 30.2)
HAVE_LEFT = (20.0, 28.5, 37.0, 40.0)


def ring_order(direction):
    hops = HOPS[direction]
    done = dict.fromkeys(hops, 0)
    ready = dict.fromkeys(hops, 0.0)
    order, now = [], 0.0
    while done != hops:
        left = [u for u in PIECES if done[u] < hops[u]]
        now = max(now, min(ready[u] for u in left))
        active = [u for u in left if ready[u] <= now]
        u = min(active, key=lambda u: (DEADLINES[u[0]] - (SLOT + LATENCY) * (hops[u] - done[u] - 1), u))
        done[u] += 1
        order.append((now, u, done[u]))
        now += SLOT
        ready[u] = now + LATENCY
    return order


def build_events():
    events = []
    complete = [0.0] * len(PARTS)
    for direction in ("R", "L"):
        arrived = {}
        for now, u, hop in ring_order(direction):
            events.append((max(now - SLOT, arrived.get(u, 0.0)), 1, now, ("send", direction, u, hop)))
            arrived[u] = now + SLOT + LATENCY
        for u, when in arrived.items():
            events.append((when, 0, when, ("land", direction, u, HOPS[direction][u])))
            complete[u[0]] = max(complete[u[0]], when)
    for p in range(len(PARTS)):
        events.append((1.5 * STARTS[p] / 64, 2, p, ("share", p)))
        for h in range(STAGES):
            events.append((max(complete[p] + 1.0, HAVE_LEFT[h]), 4, h, ("block", p, h)))
    for h in range(STAGES):
        events.append((SEND_LEFT[h], 3, h, ("left", h)))
        events.append((PASS_LEFT[h], 3, h, ("pass", h)))
    return [e[3] for e in sorted(events, key=lambda e: e[:3])]


def kernel(
    rows_hbm, slab_hbm, pattern_hbm, kept_hbm, fill_hbm, out_ref,
    rows, slab, pattern, kept, fill, left, in_sem, scalar_sem, left_send, left_recv,
    ring_send, ring_recv, pair_send, pair_recv, sum_send, sum_recv, *buffers,
):
    count_parts = len(PARTS)
    right, partial, landed = (buffers[i * count_parts:(i + 1) * count_parts] for i in range(3))
    r, c, l = (lax.axis_index(name) for name in ("row", "col", "layer"))
    core = lax.rem(c, 2)
    sibling = (r, c + 1 - 2 * core, l)
    ring = {"R": (r, lax.rem(c + 2, TILES), l), "L": (r, lax.rem(c + TILES - 2, TILES), l)}
    row_ring = [(lax.rem(r + o, RUNS), c, l) for o in (1, RUNS - 1)]
    row_from = [lax.rem(r + o, RUNS) for o in (RUNS - 1, 1)]
    layer_mates = [(r, c, lax.rem(l + o, LAYERS)) for o in OFFSETS[:-1]]

    slab_copy = pltpu.make_async_copy(slab_hbm.at[0], slab, in_sem.at[PER_RUN])
    scalar_copies = [
        pltpu.make_async_copy(pattern_hbm, pattern, scalar_sem.at[0]),
        pltpu.make_async_copy(kept_hbm, kept, scalar_sem.at[1]),
        pltpu.make_async_copy(fill_hbm, fill, scalar_sem.at[2]),
    ]
    tile_copies = [
        pltpu.make_async_copy(rows_hbm.at[0, :, pl.ds(t * TILE, TILE)], rows.at[t], in_sem.at[t])
        for t in range(PER_RUN)
    ]
    for copy in scalar_copies + [slab_copy] + tile_copies:
        copy.start()

    barrier = pltpu.get_barrier_semaphore()
    mates = layer_mates + row_ring + [ring["R"], ring["L"], sibling]
    for mate in mates:
        pl.semaphore_signal(barrier, inc=1, device_id=mate, device_id_type=MESH)

    for copy in scalar_copies:
        copy.wait()
    picks = []
    for g in range(RUNS):
        bits = [pattern[0, 0, g * PER_RUN + t] > 0 for t in range(PER_RUN)]
        first = jnp.where(bits[0], 0, jnp.where(bits[1], 1, jnp.where(bits[2], 2, 3)))
        final = jnp.where(bits[3], 3, jnp.where(bits[2], 2, jnp.where(bits[1], 1, 0)))
        picks.append((g * PER_RUN + first, g * PER_RUN + final))
    own = [pattern[0, 0, r * PER_RUN + t] for t in range(PER_RUN)]
    count = own[0] + own[1] + own[2] + own[3]
    own_first = jnp.where(own[0] > 0, 0, jnp.where(own[1] > 0, 1, jnp.where(own[2] > 0, 2, 3)))
    own_final = jnp.where(own[3] > 0, 3, jnp.where(own[2] > 0, 2, jnp.where(own[1] > 0, 1, 0)))

    slab_copy.wait()
    limit = jnp.where(kept[0, 0, 0] > 0, fill[0, 0], 0)
    live = lax.broadcasted_iota(jnp.int32, (TILE, LANES), 0) < limit
    low = lax.broadcasted_iota(jnp.int32, (DEPTH, LANES), 1) < 64

    def swap(x):
        return pltpu.roll(x, 64, 1)

    for p, width in enumerate(PARTS):
        base = STARTS[p] // LANES * LANES
        piece = jnp.where(live, slab[:, base:base + LANES].astype(jnp.float32), 0.0)
        if width == 64:
            top, bottom = piece[:DEPTH], piece[DEPTH:]
            piece = jnp.where(low, top, swap(bottom)) if STARTS[p] == base else jnp.where(low, swap(top), bottom)
        right[p][c] = piece.astype(jnp.bfloat16)

    pl.semaphore_wait(barrier, len(mates))

    hop_list = [(d, u, h) for d in ("R", "L") for u in PIECES for h in range(1, HOPS[d][u] + 1)]
    number = {piece: i for i, piece in enumerate(hop_list)}

    def piece_view(direction, u, hops):
        tile = lax.rem(c + (TILES - 2 * hops if direction == "R" else 2 * hops), TILES)
        return right[u[0]].at[tile, pl.ds(u[1] * DEPTH, DEPTH)]

    def to_sibling(p, view):
        pltpu.make_async_remote_copy(
            src_ref=view, dst_ref=view, send_sem=pair_send.at[p], recv_sem=pair_recv.at[p],
            device_id=sibling, device_id_type=MESH).start()

    def hop_copy(direction, u, hop):
        view = piece_view(direction, u, hop - 1)
        return pltpu.make_async_remote_copy(
            src_ref=view, dst_ref=view, send_sem=ring_send.at[0 if direction == "R" else 1],
            recv_sem=ring_recv.at[number[direction, u, hop]], device_id=ring[direction], device_id_type=MESH)

    def arrive(direction, u, hop):
        view = piece_view(direction, u, hop)
        pltpu.make_async_copy(view, view, ring_recv.at[number[direction, u, hop]]).wait()
        return view

    def fill_stage(h):
        for slot, (tile, least) in enumerate(((own_first, 1), (own_final, 2))):
            weight = jnp.full((OWNED, TILE), jnp.where(count >= least, 1.0, 0.0), jnp.float32).astype(jnp.bfloat16)
            for half in range(2):
                first_row = pl.multiple_of(lax.rem(l + OFFSETS[2 * h + half], LAYERS) * OWNED, OWNED)
                piece = rows[tile, pl.ds(first_row, OWNED), :]
                left[h, r, slot, half * OWNED:(half + 1) * OWNED, :] = piece * weight

    def left_copy(h, way):
        view = left.at[h, r]
        return pltpu.make_async_remote_copy(
            src_ref=view, dst_ref=view, send_sem=left_send.at[h], recv_sem=left_recv.at[h, way],
            device_id=row_ring[way], device_id_type=MESH)

    def pass_copy(h, way):
        view = left.at[h, row_from[way], way]
        return pltpu.make_async_remote_copy(
            src_ref=view, dst_ref=view, send_sem=left_send.at[h], recv_sem=left_recv.at[h, 2],
            device_id=row_ring[way], device_id_type=MESH)

    have_rows, have_left, have_right = False, set(), set()
    for step in build_events():
        if step[0] == "send":
            _, direction, u, hop = step
            view = arrive(direction, u, hop - 1) if hop > 1 else None
            hop_copy(direction, u, hop).start()
            if view is not None:
                to_sibling(u[0], view)
        elif step[0] == "land":
            to_sibling(step[2][0], arrive(*step[1:]))
        elif step[0] == "share":
            to_sibling(step[1], right[step[1]].at[c])
        elif step[0] == "left":
            if not have_rows:
                have_rows = True
                for copy in tile_copies:
                    copy.wait()
            fill_stage(step[1])
            for way in range(2):
                left_copy(step[1], way).start()
        elif step[0] == "pass":
            for way in range(2):
                view = left.at[step[1], row_from[way]]
                pltpu.make_async_copy(view, view, left_recv.at[step[1], way]).wait()
                pass_copy(step[1], way).start()
        else:
            _, p, h = step
            if p not in have_right:
                have_right.add(p)
                view = right[p].at[pl.ds(0, TILES // 2)]
                pltpu.make_async_copy(view, view, pair_recv.at[p]).wait()
            if h not in have_left:
                have_left.add(h)
                view = left.at[h, 0]
                pltpu.make_async_copy(view, view, left_recv.at[h, 2]).wait()
            totals = [None, None]
            for g in range(RUNS):
                for slot in range(SLOTS):
                    tile = right[p][picks[g][slot]]
                    if PARTS[p] == LANES:
                        terms = [jnp.dot(left[h, g, slot], tile, preferred_element_type=jnp.float32)]
                    else:
                        terms = [
                            jnp.dot(left[h, g, slot, :, :DEPTH], tile, preferred_element_type=jnp.float32),
                            jnp.dot(left[h, g, slot, :, DEPTH:], tile, preferred_element_type=jnp.float32),
                        ]
                    for i, term in enumerate(terms):
                        totals[i] = term if totals[i] is None else totals[i] + term
            if PARTS[p] == LANES:
                partial[p][h] = totals[0].reshape(2, OWNED, LANES)
            else:
                in_low = totals[0] + swap(totals[1])
                in_high = swap(totals[0]) + totals[1]
                for half in range(2):
                    row = half * OWNED
                    partial[p][h, half] = jnp.where(
                        low[:OWNED // 2], in_low[row:row + OWNED // 2], in_high[row + OWNED // 2:row + OWNED])
            for half in range(2):
                k = 2 * h + half
                if OFFSETS[k] != 0:
                    pltpu.make_async_remote_copy(
                        src_ref=partial[p].at[h, half], dst_ref=landed[p].at[k],
                        send_sem=sum_send.at[p], recv_sem=sum_recv.at[p],
                        device_id=layer_mates[k], device_id_type=MESH).start()

    def drain(view, sem):
        pltpu.make_async_copy(view, view, sem).wait()

    for i in range(2):
        drain(right[0].at[pl.ds(0, TILES - 2)], ring_send.at[i])
    for h in range(STAGES):
        drain(left.at[h, pl.ds(0, RUNS - 1)], left_send.at[h])
    for p in range(count_parts):
        drain(right[p].at[pl.ds(0, TILES // 2)], pair_send.at[p])
    sums = []
    for p in range(count_parts):
        drain(landed[p], sum_recv.at[p])
        total = partial[p][STAGES - 1, 1]
        for k in range(LAYERS - 1):
            total = total + landed[p][k]
        sums.append(total)
        base = STARTS[p] // LANES * LANES
        if PARTS[p] == LANES:
            out_ref[:, base:base + LANES] = total
        elif STARTS[p] > base:
            one, two = sums[p - 1], sums[p]
            out_ref[:OWNED // 2, base:base + LANES] = jnp.where(low[:OWNED // 2], one, swap(two))
            out_ref[OWNED // 2:, base:base + LANES] = jnp.where(low[:OWNED // 2], swap(one), two)
    for p in range(count_parts):
        drain(landed[p], sum_send.at[p])


def body(iterate_rows, square_slab, row_pattern, slab_pattern, fill_counts, iterate_slab):
    in_hbm = pl.BlockSpec(memory_space=pltpu.HBM)
    dma = pltpu.SemaphoreType.DMA
    parts = len(PARTS)
    deep = [width // 64 for width in PARTS]
    product = pl.pallas_call(
        kernel,
        out_shape=jax.ShapeDtypeStruct((OWNED, TILE), jnp.float32),
        in_specs=[in_hbm] * 5,
        out_specs=pl.BlockSpec(memory_space=pltpu.VMEM),
        scratch_shapes=[
            pltpu.VMEM((PER_RUN, TILE, TILE), jnp.bfloat16),
            pltpu.VMEM((TILE, TILE), jnp.bfloat16),
            pltpu.SMEM((1, 1, TILES), jnp.int32),
            pltpu.SMEM((1, 1, 1), jnp.int32),
            pltpu.SMEM((1, 1), jnp.int32),
            pltpu.VMEM((STAGES, RUNS, SLOTS, STAGE_ROWS, TILE), jnp.bfloat16),
            dma((PER_RUN + 1,)), dma((3,)),
            dma((STAGES,)), dma((STAGES, 3)),
            dma((2,)), dma((len(PIECES) * (CHIPS - 1),)),
            dma((parts,)), dma((parts,)), dma((parts,)), dma((parts,)),
        ]
        + [pltpu.VMEM((TILES, d * DEPTH, LANES), jnp.bfloat16) for d in deep]
        + [pltpu.VMEM((STAGES, 2, d * OWNED // 2, LANES), jnp.float32) for d in deep]
        + [pltpu.VMEM((LAYERS - 1, d * OWNED // 2, LANES), jnp.float32) for d in deep],
        compiler_params=pltpu.CompilerParams(
            collective_id=0, has_side_effects=True, vmem_limit_bytes=60 << 20),
        name="sparse_product",
    )(iterate_rows, square_slab, row_pattern, slab_pattern, fill_counts)
    return 1.5 * iterate_slab - 0.5 * product


def solution(mesh):
    return jax.shard_map(
        body,
        mesh=mesh,
        in_specs=(
            P("layer", "col", "row"),
            P("layer", "col", "row"),
            P("layer", "col", None),
            P("layer", "col", "row"),
            P("layer", "col"),
            P(("col", "layer"), "row"),
        ),
        out_specs=P(("col", "layer"), "row"),
        check_vma=False,
    )
```

time: 226 us -> 72.4 us (0.32); the launches traced: 221 us -> 72.2 us
  waiting for transfers between devices: 188 us -> 0 us
  Pallas kernels: 0 us -> 69.3 us
  between operations: 14.4 us -> 1.35 us
  matrix products: 9.55 us -> 0 us
  local copies, waits for them, and re-layouts: 5.22 us -> 0.01 us
  other arithmetic: 4.22 us -> 1.58 us
    all_gather x2 -> x0, waiting for transfers between devices: 152 us -> none  [the longest x1 90 us: body(): lax.all_gather(iterate_rows, 'row', axis=2, tiled=True)[0]]
    pallas_call x0 -> x1, Pallas kernels: none -> 69.3 us  [body(): pl.pallas_call(kernel, out_shape=jax.ShapeDtypeStruct((OWNED, TILE), jnp....]
    reduce_scatter x1 -> x0, waiting for transfers between devices: 35.9 us -> none  [body(): lax.psum_scatter(partial_sum, 'layer', scatter_dimension=0, tiled=True)]
    dot_general x1 -> x0, matrix products: 9.55 us -> none  [body(): jnp.einsum('itk,tkj->ij', row_tiles, right, preferred_element_type=jnp.fl...]
    unnamed x4 -> x2, local copies, waits for them, and re-layouts: 5.22 us -> 0.01 us
  transfers between devices with their start and end apart: 3 -> 0, of which waited for: 3 -> 0; matrix products, arithmetic and copies ran while one was open for 1% -> 0% of each run, Pallas kernels for 0% -> 0%
where the time goes in v2:
time: 72.4 us; the launch traced here: 72.2 us
  Pallas kernels  69.3 us (96%)
  other arithmetic  1.58 us (2%)
  between operations  1.35 us (2%)
    pallas_call x1, Pallas kernels, body(): pl.pallas_call(kernel, out_shape=jax.ShapeDtypeStruct((OWNED, TILE), jnp....  69.3 us
    sub x1, other arithmetic, body(): return 1.5 * iterate_slab - 0.5 * product  1.58 us

profile of v2, /device:TPU:1, one launch (start us, length us, event | category | flops | bytes accessed | tf_op | source)
XLA Modules:
  0.0 72.2 jit_solution(16621074131827081794)
XLA Ops:
  0.0 0.0 copy-start
  1.3 69.3 %sparse_product.1 = f32[64,512]{1,0:T(8,128)} custom-call(bf16[1,512,2048]{2,1,0:T(8,128)(2,1)} %rows_hbm.1, bf16[1,512,512]{2,1,0:T(8,128)(2,1)} %slab_hbm.1, s32[1,1,16]{2,1,0:T(1,128)} %pattern_hbm.1, s32[1,1,1]{2,1,0:T(1,128)S(6)} %copy.7.kept_hbm, s32[1,1]{1,0:T(1,128)S(6)} %copy.8.fill_hbm), custom_call_target="tpu_custom_call" | custom-call | tf_op jit(solution)/shard_map/sparse_product/pallas_call | solution.py:282
  70.7 0.0 copy-done
  70.7 1.6 %multiply_subtract_fusion = f32[64,512]{1,0:T(8,128)} fusion(f32[64,512]{1,0:T(8,128)} %sparse_product.1, f32[64,512]{1,0:T(8,128)S(1)} %copy-done), kind=kLoop, calls=%fused_computation | loop fusion | flops 98304 | bytes 393216 | tf_op jit(solution)/shard_map/sub | solution.py:306
Async XLA Ops:
  0.0 70.7 %copy-start = (f32[64,512]{1,0:T(8,128)S(1)}, f32[64,512]{1,0:T(8,128)}, u32[]{:S(2)}) copy-start(f32[64,512]{1,0:T(8,128)} %param.11) | copy-start | bytes 393220

commit v3 on v2

--- a/solution.py
+++ b/solution.py
@@ -35,6 +35,7 @@
 SEND_LEFT = (0.0, 0.0, 8.3, 13.8)
 PASS_LEFT = (8.2, 13.7, 22.0, 30.2)
 HAVE_LEFT = (20.0, 28.5, 37.0, 40.0)
+GREET = (10.0, 14.0, 17.0, 19.0)
 
 
 def ring_order(direction):
@@ -72,13 +73,15 @@
     for h in range(STAGES):
         events.append((SEND_LEFT[h], 3, h, ("left", h)))
         events.append((PASS_LEFT[h], 3, h, ("pass", h)))
+    for k in range(len(GREET)):
+        events.append((GREET[k], 3, k, ("greet", k)))
     return [e[3] for e in sorted(events, key=lambda e: e[:3])]
 
 
 def kernel(
-    rows_hbm, slab_hbm, pattern_hbm, kept_hbm, fill_hbm, out_ref,
-    rows, slab, pattern, kept, fill, left, in_sem, scalar_sem, left_send, left_recv,
-    ring_send, ring_recv, pair_send, pair_recv, sum_send, sum_recv, *buffers,
+    rows_hbm, slab_hbm, pattern_hbm, kept_hbm, fill_hbm, iterate_hbm, out_ref,
+    rows, slab, pattern, kept, fill, iterate, left, in_sem, scalar_sem, left_send, left_recv,
+    ring_send, ring_recv, pair_send, pair_recv, sum_send, sum_recv, greet_sem, *buffers,
 ):
     count_parts = len(PARTS)
     right, partial, landed = (buffers[i * count_parts:(i + 1) * count_parts] for i in range(3))
@@ -100,12 +103,14 @@
         pltpu.make_async_copy(rows_hbm.at[0, :, pl.ds(t * TILE, TILE)], rows.at[t], in_sem.at[t])
         for t in range(PER_RUN)
     ]
-    for copy in scalar_copies + [slab_copy] + tile_copies:
+    iterate_copy = pltpu.make_async_copy(iterate_hbm, iterate, in_sem.at[PER_RUN + 1])
+    for copy in scalar_copies + [slab_copy] + tile_copies + [iterate_copy]:
         copy.start()
 
     barrier = pltpu.get_barrier_semaphore()
-    mates = layer_mates + row_ring + [ring["R"], ring["L"], sibling]
-    for mate in mates:
+    above, below = (r, c, lax.rem(l + 1, LAYERS)), (r, c, lax.rem(l + LAYERS - 1, LAYERS))
+    mates = row_ring + [ring["R"], ring["L"], sibling]
+    for mate in mates + [below]:
         pl.semaphore_signal(barrier, inc=1, device_id=mate, device_id_type=MESH)
 
     for copy in scalar_copies:
@@ -137,7 +142,8 @@
             piece = jnp.where(low, top, swap(bottom)) if STARTS[p] == base else jnp.where(low, swap(top), bottom)
         right[p][c] = piece.astype(jnp.bfloat16)
 
-    pl.semaphore_wait(barrier, len(mates))
+    pl.semaphore_wait(barrier, len(mates) + 1)
+    pl.semaphore_signal(greet_sem.at[0], inc=1, device_id=above, device_id_type=MESH)
 
     hop_list = [(d, u, h) for d in ("R", "L") for u in PIECES for h in range(1, HOPS[d][u] + 1)]
     number = {piece: i for i, piece in enumerate(hop_list)}
@@ -192,6 +198,12 @@
                 to_sibling(u[0], view)
         elif step[0] == "land":
             to_sibling(step[2][0], arrive(*step[1:]))
+        elif step[0] == "greet":
+            k = step[1]
+            pl.semaphore_wait(greet_sem.at[k], 1 if k == 0 else 2)
+            if k + 1 < len(GREET):
+                for mate in (above, below):
+                    pl.semaphore_signal(greet_sem.at[k + 1], inc=1, device_id=mate, device_id_type=MESH)
         elif step[0] == "share":
             to_sibling(step[1], right[step[1]].at[c])
         elif step[0] == "left":
@@ -256,7 +268,13 @@
         drain(left.at[h, pl.ds(0, RUNS - 1)], left_send.at[h])
     for p in range(count_parts):
         drain(right[p].at[pl.ds(0, TILES // 2)], pair_send.at[p])
+    iterate_copy.wait()
     sums = []
+
+    def finish(first_row, last_row, base, total):
+        out_ref[first_row:last_row, base:base + LANES] = (
+            1.5 * iterate[first_row:last_row, base:base + LANES] - 0.5 * total)
+
     for p in range(count_parts):
         drain(landed[p], sum_recv.at[p])
         total = partial[p][STAGES - 1, 1]
@@ -265,11 +283,11 @@
         sums.append(total)
         base = STARTS[p] // LANES * LANES
         if PARTS[p] == LANES:
-            out_ref[:, base:base + LANES] = total
+            finish(0, OWNED, base, total)
         elif STARTS[p] > base:
             one, two = sums[p - 1], sums[p]
-            out_ref[:OWNED // 2, base:base + LANES] = jnp.where(low[:OWNED // 2], one, swap(two))
-            out_ref[OWNED // 2:, base:base + LANES] = jnp.where(low[:OWNED // 2], swap(one), two)
+            finish(0, OWNED // 2, base, jnp.where(low[:OWNED // 2], one, swap(two)))
+            finish(OWNED // 2, OWNED, base, jnp.where(low[:OWNED // 2], swap(one), two))
     for p in range(count_parts):
         drain(landed[p], sum_send.at[p])
 
@@ -279,10 +297,10 @@
     dma = pltpu.SemaphoreType.DMA
     parts = len(PARTS)
     deep = [width // 64 for width in PARTS]
-    product = pl.pallas_call(
+    return pl.pallas_call(
         kernel,
         out_shape=jax.ShapeDtypeStruct((OWNED, TILE), jnp.float32),
-        in_specs=[in_hbm] * 5,
+        in_specs=[in_hbm] * 6,
         out_specs=pl.BlockSpec(memory_space=pltpu.VMEM),
         scratch_shapes=[
             pltpu.VMEM((PER_RUN, TILE, TILE), jnp.bfloat16),
@@ -290,11 +308,13 @@
             pltpu.SMEM((1, 1, TILES), jnp.int32),
             pltpu.SMEM((1, 1, 1), jnp.int32),
             pltpu.SMEM((1, 1), jnp.int32),
+            pltpu.VMEM((OWNED, TILE), jnp.float32),
             pltpu.VMEM((STAGES, RUNS, SLOTS, STAGE_ROWS, TILE), jnp.bfloat16),
-            dma((PER_RUN + 1,)), dma((3,)),
+            dma((PER_RUN + 2,)), dma((3,)),
             dma((STAGES,)), dma((STAGES, 3)),
             dma((2,)), dma((len(PIECES) * (CHIPS - 1),)),
             dma((parts,)), dma((parts,)), dma((parts,)), dma((parts,)),
+            pltpu.SemaphoreType.REGULAR((len(GREET),)),
         ]
         + [pltpu.VMEM((TILES, d * DEPTH, LANES), jnp.bfloat16) for d in deep]
         + [pltpu.VMEM((STAGES, 2, d * OWNED // 2, LANES), jnp.float32) for d in deep]
@@ -302,8 +322,7 @@
         compiler_params=pltpu.CompilerParams(
             collective_id=0, has_side_effects=True, vmem_limit_bytes=60 << 20),
         name="sparse_product",
-    )(iterate_rows, square_slab, row_pattern, slab_pattern, fill_counts)
-    return 1.5 * iterate_slab - 0.5 * product
+    )(iterate_rows, square_slab, row_pattern, slab_pattern, fill_counts, iterate_slab)
 
 
 def solution(mesh):

time: 72.4 us -> 70.4 us (0.972)
  Pallas kernels: 69.3 us -> 67.4 us
  other arithmetic: 1.58 us -> 0 us
  local copies, waits for them, and re-layouts: 0.01 us -> 1.57 us
    pallas_call x1, Pallas kernels: 69.3 us -> 67.4 us  [body(): pl.pallas_call(kernel, out_shape=jax.ShapeDtypeStruct((OWNED, TILE), jnp....]
    sub x1 -> x0, other arithmetic: 1.58 us -> none  [body(): return 1.5 * iterate_slab - 0.5 * product]
    unnamed x2 -> x1, local copies, waits for them, and re-layouts: 0.01 us -> 1.57 us
where the time goes in v3:
time: 70.4 us; the launch traced here: 70.2 us
  Pallas kernels  67.4 us (96%)
  local copies, waits for them, and re-layouts  1.57 us (2%)
  between operations  1.3 us (2%)
    pallas_call x1, Pallas kernels, body(): pl.pallas_call(kernel, out_shape=jax.ShapeDtypeStruct((OWNED, TILE), jnp....  67.4 us
    unnamed x1, local copies, waits for them, and re-layouts  1.57 us

profile of v3, /device:TPU:1, one launch (start us, length us, event | category | flops | bytes accessed | tf_op | source)
XLA Modules:
  0.0 70.2 jit_solution(1810611021465599251)
XLA Ops:
  1.3 67.4 %sparse_product.1 = f32[64,512]{1,0:T(8,128)} custom-call(bf16[1,512,2048]{2,1,0:T(8,128)(2,1)} %rows_hbm.1, bf16[1,512,512]{2,1,0:T(8,128)(2,1)} %slab_hbm.1, s32[1,1,16]{2,1,0:T(1,128)} %pattern_hbm.1, s32[1,1,1]{2,1,0:T(1,128)S(6)} %copy.8.kept_hbm, s32[1,1]{1,0:T(1,128)S(6)} %copy.9.fill_hbm, f32[64,512]{1,0:T(8,128)} %iterate_hbm.1), custom_call_target="tpu_custom_call" | custom-call | tf_op jit(solution)/shard_map/sparse_product/pallas_call | solution.py:300
  68.7 1.6 %copy.10 = f32[64,512]{1,0:T(8,128)} copy(f32[64,512]{1,0:T(8,128)} %sparse_product.1) | data formatting | bytes 262144

commit v4 on v3

--- a/solution.py
+++ b/solution.py
@@ -79,8 +79,8 @@
 
 
 def kernel(
-    rows_hbm, slab_hbm, pattern_hbm, kept_hbm, fill_hbm, iterate_hbm, out_ref,
-    rows, slab, pattern, kept, fill, iterate, left, in_sem, scalar_sem, left_send, left_recv,
+    rows_hbm, slab_hbm, pattern_hbm, kept_hbm, fill_hbm, out_ref,
+    rows, slab, pattern, kept, fill, left, in_sem, scalar_sem, left_send, left_recv,
     ring_send, ring_recv, pair_send, pair_recv, sum_send, sum_recv, greet_sem, *buffers,
 ):
     count_parts = len(PARTS)
@@ -103,8 +103,7 @@
         pltpu.make_async_copy(rows_hbm.at[0, :, pl.ds(t * TILE, TILE)], rows.at[t], in_sem.at[t])
         for t in range(PER_RUN)
     ]
-    iterate_copy = pltpu.make_async_copy(iterate_hbm, iterate, in_sem.at[PER_RUN + 1])
-    for copy in scalar_copies + [slab_copy] + tile_copies + [iterate_copy]:
+    for copy in scalar_copies + [slab_copy] + tile_copies:
         copy.start()
 
     barrier = pltpu.get_barrier_semaphore()
@@ -268,12 +267,11 @@
         drain(left.at[h, pl.ds(0, RUNS - 1)], left_send.at[h])
     for p in range(count_parts):
         drain(right[p].at[pl.ds(0, TILES // 2)], pair_send.at[p])
-    iterate_copy.wait()
     sums = []
 
     def finish(first_row, last_row, base, total):
         out_ref[first_row:last_row, base:base + LANES] = (
-            1.5 * iterate[first_row:last_row, base:base + LANES] - 0.5 * total)
+            total)
 
     for p in range(count_parts):
         drain(landed[p], sum_recv.at[p])
@@ -297,10 +295,10 @@
     dma = pltpu.SemaphoreType.DMA
     parts = len(PARTS)
     deep = [width // 64 for width in PARTS]
-    return pl.pallas_call(
+    product = pl.pallas_call(
         kernel,
         out_shape=jax.ShapeDtypeStruct((OWNED, TILE), jnp.float32),
-        in_specs=[in_hbm] * 6,
+        in_specs=[in_hbm] * 5,
         out_specs=pl.BlockSpec(memory_space=pltpu.VMEM),
         scratch_shapes=[
             pltpu.VMEM((PER_RUN, TILE, TILE), jnp.bfloat16),
@@ -308,7 +306,6 @@
             pltpu.SMEM((1, 1, TILES), jnp.int32),
             pltpu.SMEM((1, 1, 1), jnp.int32),
             pltpu.SMEM((1, 1), jnp.int32),
-            pltpu.VMEM((OWNED, TILE), jnp.float32),
             pltpu.VMEM((STAGES, RUNS, SLOTS, STAGE_ROWS, TILE), jnp.bfloat16),
             dma((PER_RUN + 2,)), dma((3,)),
             dma((STAGES,)), dma((STAGES, 3)),
@@ -320,9 +317,10 @@
         + [pltpu.VMEM((STAGES, 2, d * OWNED // 2, LANES), jnp.float32) for d in deep]
         + [pltpu.VMEM((LAYERS - 1, d * OWNED // 2, LANES), jnp.float32) for d in deep],
         compiler_params=pltpu.CompilerParams(
-            collective_id=0, has_side_effects=True, vmem_limit_bytes=60 << 20),
+            collective_id=0, has_side_effects=True, vmem_limit_bytes=55000 << 10),
         name="sparse_product",
-    )(iterate_rows, square_slab, row_pattern, slab_pattern, fill_counts, iterate_slab)
+    )(iterate_rows, square_slab, row_pattern, slab_pattern, fill_counts)
+    return 1.5 * iterate_slab - 0.5 * product
 
 
 def solution(mesh):

time: 70.4 us -> 69.7 us (0.990)
  local copies, waits for them, and re-layouts: 1.57 us -> 0.65 us
    unnamed x1 -> x4, local copies, waits for them, and re-layouts: 1.57 us -> 0.65 us
where the time goes in v4:
time: 69.7 us; the launch traced here: 69.5 us
  Pallas kernels  66.8 us (96%)
  between operations  1.32 us (2%)
    pallas_call x1, Pallas kernels, body(): pl.pallas_call(kernel, out_shape=jax.ShapeDtypeStruct((OWNED, TILE), jnp....  66.8 us

profile of v4, /device:TPU:1, one launch (start us, length us, event | category | flops | bytes accessed | tf_op | source)
XLA Modules:
  0.0 69.5 jit_solution(9759038996157294241)
XLA Ops:
  1.3 0.0 copy-start
  1.3 0.6 copy-done
  2.0 0.0 copy-start.1
  2.0 66.8 %sparse_product.1 = f32[64,512]{1,0:T(8,128)S(1)} custom-call(bf16[1,512,2048]{2,1,0:T(8,128)(2,1)} %rows_hbm.1, bf16[1,512,512]{2,1,0:T(8,128)(2,1)} %slab_hbm.1, s32[1,1,16]{2,1,0:T(1,128)S(1)} %copy-done, s32[1,1,1]{2,1,0:T(1,128)S(6)} %copy.7.kept_hbm, s32[1,1]{1,0:T(1,128)S(6)} %copy.8.fill_hbm), custom_call_target="tpu_custom_call" | custom-call | tf_op jit(solution)/shard_map/sparse_product/pallas_call | solution.py:298
  68.8 0.0 copy-done.1
  68.8 0.7 multiply_subtract_fusion
Async XLA Ops:
  1.3 0.7 copy-start
  2.0 66.9 %copy-start.1 = (f32[64,512]{1,0:T(8,128)S(1)}, f32[64,512]{1,0:T(8,128)}, u32[]{:S(2)}) copy-start(f32[64,512]{1,0:T(8,128)} %param.11) | copy-start | bytes 393220

commit v5 on v4

--- a/solution.py
+++ b/solution.py
@@ -31,10 +31,10 @@
 
 SLOT = 1.4
 LATENCY = 2.7
-DEADLINES = (21, 23, 25, 33, 35, 38)
+DEADLINES = (20, 23, 26, 32, 34, 37)
 SEND_LEFT = (0.0, 0.0, 8.3, 13.8)
 PASS_LEFT = (8.2, 13.7, 22.0, 30.2)
-HAVE_LEFT = (20.0, 28.5, 37.0, 40.0)
+HAVE_LEFT = (17.0, 25.5, 34.0, 37.0)
 GREET = (10.0, 14.0, 17.0, 19.0)
 
 
@@ -69,7 +69,7 @@
     for p in range(len(PARTS)):
         events.append((1.5 * STARTS[p] / 64, 2, p, ("share", p)))
         for h in range(STAGES):
-            events.append((max(complete[p] + 1.0, HAVE_LEFT[h]), 4, h, ("block", p, h)))
+            events.append((max(complete[p] + 2.0, HAVE_LEFT[h]), 4, h, ("block", p, h)))
     for h in range(STAGES):
         events.append((SEND_LEFT[h], 3, h, ("left", h)))
         events.append((PASS_LEFT[h], 3, h, ("pass", h)))

time: 69.7 us -> 68 us (0.976)
  Pallas kernels: 66.8 us -> 65.2 us
    pallas_call x1, Pallas kernels: 66.8 us -> 65.2 us  [body(): pl.pallas_call(kernel, out_shape=jax.ShapeDtypeStruct((OWNED, TILE), jnp....]
where the time goes in v5:
time: 68 us; the launch traced here: 67.8 us
  Pallas kernels  65.2 us (96%)
  between operations  1.32 us (2%)
  other arithmetic  0.68 us (1%)
    pallas_call x1, Pallas kernels, body(): pl.pallas_call(kernel, out_shape=jax.ShapeDtypeStruct((OWNED, TILE), jnp....  65.2 us

profile of v5, /device:TPU:1, one launch (start us, length us, event | category | flops | bytes accessed | tf_op | source)
XLA Modules:
  0.0 67.8 jit_solution(5242547617550907130)
XLA Ops:
  1.3 0.0 copy-start
  1.3 0.6 copy-done
  2.0 0.0 copy-start.1
  2.0 65.2 %sparse_product.1 = f32[64,512]{1,0:T(8,128)S(1)} custom-call(bf16[1,512,2048]{2,1,0:T(8,128)(2,1)} %rows_hbm.1, bf16[1,512,512]{2,1,0:T(8,128)(2,1)} %slab_hbm.1, s32[1,1,16]{2,1,0:T(1,128)S(1)} %copy-done, s32[1,1,1]{2,1,0:T(1,128)S(6)} %copy.7.kept_hbm, s32[1,1]{1,0:T(1,128)S(6)} %copy.8.fill_hbm), custom_call_target="tpu_custom_call" | custom-call | tf_op jit(solution)/shard_map/sparse_product/pallas_call | solution.py:298
  67.1 0.0 copy-done.1
  67.2 0.7 multiply_subtract_fusion
Async XLA Ops:
  1.3 0.7 copy-start
  2.0 65.2 %copy-start.1 = (f32[64,512]{1,0:T(8,128)S(1)}, f32[64,512]{1,0:T(8,128)}, u32[]{:S(2)}) copy-start(f32[64,512]{1,0:T(8,128)} %param.11) | copy-start | bytes 393220

commit v6 on v5

--- a/solution.py
+++ b/solution.py
@@ -35,7 +35,7 @@
 SEND_LEFT = (0.0, 0.0, 8.3, 13.8)
 PASS_LEFT = (8.2, 13.7, 22.0, 30.2)
 HAVE_LEFT = (17.0, 25.5, 34.0, 37.0)
-GREET = (10.0, 14.0, 17.0, 19.0)
+GREET = (5.5, 11.0, 16.0, 20.5)
 
 
 def ring_order(direction):

time: 68 us -> 68 us (level)
  no operation moved by 1% of the time
where the time goes in v6:
time: 68 us; the launch traced here: 67.8 us
  Pallas kernels  65.2 us (96%)
  between operations  1.32 us (2%)
  other arithmetic  0.68 us (1%)
    pallas_call x1, Pallas kernels, body(): pl.pallas_call(kernel, out_shape=jax.ShapeDtypeStruct((OWNED, TILE), jnp....  65.2 us

profile of v6, /device:TPU:1, one launch (start us, length us, event | category | flops | bytes accessed | tf_op | source)
XLA Modules:
  0.0 67.8 jit_solution(16415758297329735478)
XLA Ops:
  1.3 0.0 copy-start
  1.3 0.6 copy-done
  2.0 0.0 copy-start.1
  2.0 65.2 %sparse_product.1 = f32[64,512]{1,0:T(8,128)S(1)} custom-call(bf16[1,512,2048]{2,1,0:T(8,128)(2,1)} %rows_hbm.1, bf16[1,512,512]{2,1,0:T(8,128)(2,1)} %slab_hbm.1, s32[1,1,16]{2,1,0:T(1,128)S(1)} %copy-done, s32[1,1,1]{2,1,0:T(1,128)S(6)} %copy.7.kept_hbm, s32[1,1]{1,0:T(1,128)S(6)} %copy.8.fill_hbm), custom_call_target="tpu_custom_call" | custom-call | tf_op jit(solution)/shard_map/sparse_product/pallas_call | solution.py:298
  67.1 0.0 copy-done.1
  67.2 0.7 multiply_subtract_fusion
Async XLA Ops:
  1.3 0.7 copy-start
  2.0 65.2 %copy-start.1 = (f32[64,512]{1,0:T(8,128)S(1)}, f32[64,512]{1,0:T(8,128)}, u32[]{:S(2)}) copy-start(f32[64,512]{1,0:T(8,128)} %param.11) | copy-start | bytes 393220
